TPU v7x, 32 devices: a whole 2x2x4 slice. The times are simulated.
32 devices in a mesh: grp: 2 (over x), col: 16 (over z, y, core).
Axes of the slice: x: 2, y: 2, z: 4, core: 2. Of those that a mesh axis runs over, the one named last changes fastest.
Arguments:
- adjoint_in: bfloat16 [768, 137, 128], P(('grp', 'col')), parts along dimension 0, may hold values from -6 to 6
- vertical: bfloat16 [768, 137, 137], P(('grp', 'col')), parts along dimension 0, may hold values from -0.5 to 0.5
- tiles: bfloat16 [768, 8, 128, 128], P(('grp', 'col')), parts along dimension 0, may hold values from -0.5 to 0.5
- sources: int32 [768, 8], P(('grp', 'col')), parts along dimension 0, may hold values from 0 to 383, as said below
- lengths: int32 [768], P(('grp', 'col')), parts along dimension 0, may hold values from 1 to 8, as said below
- prior: float32 [768, 137, 128], P(('grp', 'col')), parts along dimension 0, may hold values from -6 to 6
Outputs:
- adjoint_out: float32 [768, 137, 128], P(('grp', 'col')), parts along dimension 0
There are 2 independent parts, one for each index of `grp`. A program takes and returns all parts, laid end to end along the dimension named above; each array names one. Nothing has to cross between parts.
Inputs may be any that keep to these rules, and one draw needn't show every extreme that they name: `sources`: each entry lies within 24 blocks of its arrival block, counted cyclically over the 384 blocks; some entry lies exactly 24 blocks ahead and some exactly 24 blocks behind. `lengths`: A run of 48 cyclically consecutive blocks has full lists.
All inputs are finite; a program needn't handle non-finite values.
Results may differ from a plain program's by a relative error of at most 0.0026.
Values may be sent and summed in bfloat16 or wider, within the bound.
A program may use at most 128 MiB of HBM per device.

v0:
```python
import jax
import jax.numpy as jnp
from jax import lax
from jax.sharding import PartitionSpec as P


def from_behind(value, axis, steps):
    count = lax.axis_size(axis)
    pairs = [(source, (source + steps) % count) for source in range(count)]
    return lax.ppermute(value, axis, pairs)


def deposit(running, products, slot_column, kept_column):
    masked = jnp.where(kept_column[:, None, None], products, jnp.zeros_like(products))
    return running.at[slot_column].add(masked)


def one_entry(running, lifted, tile_column, slot_column, kept_column):
    products = jnp.einsum("tlb,tbc->tlc", lifted, tile_column, preferred_element_type=jnp.float32)
    return deposit(running, products, slot_column, kept_column)


def accumulate(running, lifted, tiles, slot_ids, chosen):
    listed = tiles.shape[1]
    for entry in range(listed):
        tile_column = tiles[:, entry]
        slot_column = slot_ids[:, entry]
        kept_column = chosen[:, entry]
        running = one_entry(running, lifted, tile_column, slot_column, kept_column)
    return running


def exchange_rims(running, blocks_here):
    lower_part = running[:blocks_here]
    upper_part = running[2 * blocks_here :]
    from_right = from_behind(lower_part, "col", -1)
    from_left = from_behind(upper_part, "col", 1)
    return (from_right, from_left)


def local(adjoint_in, vertical, tiles, sources, lengths, prior):
    blocks_here = adjoint_in.shape[0]
    listed = tiles.shape[1]
    everywhere = lax.axis_size("col") * blocks_here
    first_block = lax.axis_index("col") * blocks_here
    lifted = jnp.einsum(
        "tml,tmb->tlb", vertical, adjoint_in, preferred_element_type=jnp.float32
    ).astype(jnp.bfloat16)
    entries = jnp.arange(listed, dtype=jnp.int32)[None, :]
    live = entries < lengths[:, None]
    offset = (sources - first_block + everywhere) % everywhere
    offset = jnp.where(offset >= everywhere - blocks_here, offset - everywhere, offset)
    slot_ids = offset + blocks_here
    empty = jnp.zeros((3 * blocks_here,) + adjoint_in.shape[1:], jnp.float32)
    running = accumulate(empty, lifted, tiles, slot_ids, live)
    from_right, from_left = exchange_rims(running, blocks_here)
    middle = running[blocks_here : 2 * blocks_here]
    return prior + middle + from_right + from_left


def solution(mesh):
    placed = (
        P(("grp", "col"), None, None),
        P(("grp", "col"), None, None),
        P(("grp", "col"), None, None, None),
        P(("grp", "col"), None),
        P(("grp", "col")),
        P(("grp", "col"), None, None),
    )
    return jax.shard_map(
        local, mesh=mesh, in_specs=placed, out_specs=P(("grp", "col"), None, None), check_vma=False
    )
```

profile of v0, /device:TPU:1, one launch (start us, length us, event | category | flops | bytes accessed | tf_op | source)
XLA Modules:
  0.0 123.9 jit_solution(5636086794799677381)
XLA Ops:
  0.0 0.0 copy-start
  0.0 0.7 iota_compare_fusion
  0.8 0.7 fusion.24
  1.5 0.0 copy-done
  1.5 0.0 copy-start.1
  1.5 2.6 %fusion.4 = bf16[24,137,128]{2,1,0:T(8,128)(2,1)S(1)} fusion(bf16[24,137,137]{2,0,1:T(8,128)(2,1)} %param.7, bf16[24,137,128]{2,0,1:T(8,128)(2,1)S(1)} %copy-done), kind=kOutput, calls=%fused_computation.21 | convolution fusion | flops 115737600 | bytes 2584368 | tf_op jit(solution)/shard_map/tml,tmb->tlb/dot_general | solution.py:46
  4.1 3.0 %convolution_select_fusion.7 = f32[24,137,128]{2,1,0:T(8,128)} fusion(bf16[24,137,128]{2,1,0:T(8,128)(2,1)S(1)} %fusion.4, pred[24]{0:T(512)(128)(4,1)S(1)} %get-tuple-element.23, bf16[24,8,128,128]{3,2,1,0:T(8,128)(2,1)} %param.8), kind=kOutput, calls=%fused_computation.20 | convolution fusion | flops 108162048 | bytes 3311640 | tf_op jit(solution)/shard_map/tlb,tbc->tlc/dot_general | solution.py:19
  7.1 0.0 copy-done.1
  7.1 1.8 %convolution_select_fusion.6 = f32[24,137,128]{2,1,0:T(8,128)} fusion(bf16[24,137,128]{2,1,0:T(8,128)(2,1)S(1)} %fusion.4, pred[24]{0:T(512)(128)(4,1)S(1)} %get-tuple-element.22, bf16[24,8,128,128]{3,2,1,0:T(8,128)(2,1)S(1)} %copy-done.1), kind=kOutput, calls=%fused_computation.19 | convolution fusion | flops 108162048 | bytes 3355136 | tf_op jit(solution)/shard_map/tlb,tbc->tlc/dot_general | solution.py:19
  8.9 1.9 %convolution_select_fusion.5 = f32[24,137,128]{2,1,0:T(8,128)} fusion(bf16[24,137,128]{2,1,0:T(8,128)(2,1)S(1)} %fusion.4, pred[24]{0:T(512)(128)(4,1)S(1)} %get-tuple-element.21, bf16[24,8,128,128]{3,2,1,0:T(8,128)(2,1)S(1)} %copy-done.1), kind=kOutput, calls=%fused_computation.18 | convolution fusion | flops 108162048 | bytes 3355136 | tf_op jit(solution)/shard_map/tlb,tbc->tlc/dot_general | solution.py:19
  10.8 1.8 %convolution_select_fusion.4 = f32[24,137,128]{2,1,0:T(8,128)} fusion(bf16[24,137,128]{2,1,0:T(8,128)(2,1)S(1)} %fusion.4, pred[24]{0:T(512)(128)(4,1)S(1)} %get-tuple-element.20, bf16[24,8,128,128]{3,2,1,0:T(8,128)(2,1)S(1)} %copy-done.1), kind=kOutput, calls=%fused_computation.17 | convolution fusion | flops 108162048 | bytes 3355136 | tf_op jit(solution)/shard_map/tlb,tbc->tlc/dot_general | solution.py:19
  12.6 1.9 %convolution_select_fusion.3 = f32[24,137,128]{2,1,0:T(8,128)} fusion(bf16[24,137,128]{2,1,0:T(8,128)(2,1)S(1)} %fusion.4, pred[24]{0:T(512)(128)(4,1)S(1)} %get-tuple-element.19, bf16[24,8,128,128]{3,2,1,0:T(8,128)(2,1)S(1)} %copy-done.1), kind=kOutput, calls=%fused_computation.16 | convolution fusion | flops 108162048 | bytes 3355136 | tf_op jit(solution)/shard_map/tlb,tbc->tlc/dot_general | solution.py:19
  14.4 1.9 %convolution_select_fusion.2 = f32[24,137,128]{2,1,0:T(8,128)} fusion(bf16[24,137,128]{2,1,0:T(8,128)(2,1)S(1)} %fusion.4, pred[24]{0:T(512)(128)(4,1)S(1)} %get-tuple-element.18, bf16[24,8,128,128]{3,2,1,0:T(8,128)(2,1)S(1)} %copy-done.1), kind=kOutput, calls=%fused_computation.15 | convolution fusion | flops 108162048 | bytes 3355136 | tf_op jit(solution)/shard_map/tlb,tbc->tlc/dot_general | solution.py:19
  16.4 1.9 %convolution_select_fusion.1 = f32[24,137,128]{2,1,0:T(8,128)} fusion(bf16[24,137,128]{2,1,0:T(8,128)(2,1)S(1)} %fusion.4, pred[24]{0:T(512)(128)(4,1)S(1)} %get-tuple-element.17, bf16[24,8,128,128]{3,2,1,0:T(8,128)(2,1)S(1)} %copy-done.1), kind=kOutput, calls=%fused_computation.14 | convolution fusion | flops 108162048 | bytes 3355136 | tf_op jit(solution)/shard_map/tlb,tbc->tlc/dot_general | solution.py:19
  18.2 0.6 convolution_select_fusion
  18.8 2.7 %broadcast_in_dim.72 = f32[72,137,128]{2,1,0:T(8,128)} broadcast(f32[]{:T(128)} %constant.8.clone.1), dimensions={} | broadcast | bytes 5050372 | tf_op jit(solution)/shard_map/broadcast_in_dim | solution.py:54
  21.5 7.3 %scatter_fusion = f32[72,137,128]{2,1,0:T(8,128)} fusion(f32[72,137,128]{2,1,0:T(8,128)} %broadcast_in_dim.72, s32[24]{0:T(128)S(1)} %get-tuple-element.15, f32[24,137,128]{2,1,0:T(8,128)} %convolution_select_fusion.7), kind=kCustom, calls=%fused_computation | custom fusion | flops 420864 | bytes 5050464 | tf_op jit(solution)/shard_map/scatter-add | solution.py:15
  28.8 7.1 %scatter_fusion.1 = f32[72,137,128]{2,1,0:T(8,128)} fusion(f32[72,137,128]{2,1,0:T(8,128)} %scatter_fusion, s32[24]{0:T(128)S(1)} %get-tuple-element.14, f32[24,137,128]{2,1,0:T(8,128)} %convolution_select_fusion.6), kind=kCustom, calls=%fused_computation.1 | custom fusion | flops 420864 | bytes 5050464 | tf_op jit(solution)/shard_map/scatter-add | solution.py:15
  35.9 7.1 %scatter_fusion.2 = f32[72,137,128]{2,1,0:T(8,128)} fusion(f32[72,137,128]{2,1,0:T(8,128)} %scatter_fusion.1, s32[24]{0:T(128)S(1)} %get-tuple-element.13, f32[24,137,128]{2,1,0:T(8,128)} %convolution_select_fusion.5), kind=kCustom, calls=%fused_computation.2 | custom fusion | flops 420864 | bytes 5050464 | tf_op jit(solution)/shard_map/scatter-add | solution.py:15
  43.1 7.0 %scatter_fusion.3 = f32[72,137,128]{2,1,0:T(8,128)} fusion(f32[72,137,128]{2,1,0:T(8,128)} %scatter_fusion.2, s32[24]{0:T(128)S(1)} %get-tuple-element.12, f32[24,137,128]{2,1,0:T(8,128)} %convolution_select_fusion.4), kind=kCustom, calls=%fused_computation.3 | custom fusion | flops 420864 | bytes 5050464 | tf_op jit(solution)/shard_map/scatter-add | solution.py:15
  50.1 7.1 %scatter_fusion.4 = f32[72,137,128]{2,1,0:T(8,128)} fusion(f32[72,137,128]{2,1,0:T(8,128)} %scatter_fusion.3, s32[24]{0:T(128)S(1)} %get-tuple-element.11, f32[24,137,128]{2,1,0:T(8,128)} %convolution_select_fusion.3), kind=kCustom, calls=%fused_computation.4 | custom fusion | flops 420864 | bytes 5050464 | tf_op jit(solution)/shard_map/scatter-add | solution.py:15
  57.2 7.1 %scatter_fusion.5 = f32[72,137,128]{2,1,0:T(8,128)} fusion(f32[72,137,128]{2,1,0:T(8,128)} %scatter_fusion.4, s32[24]{0:T(128)S(1)} %get-tuple-element.10, f32[24,137,128]{2,1,0:T(8,128)} %convolution_select_fusion.2), kind=kCustom, calls=%fused_computation.5 | custom fusion | flops 420864 | bytes 5050464 | tf_op jit(solution)/shard_map/scatter-add | solution.py:15
  64.3 7.2 %scatter_fusion.6 = f32[72,137,128]{2,1,0:T(8,128)} fusion(f32[72,137,128]{2,1,0:T(8,128)} %scatter_fusion.5, s32[24]{0:T(128)S(1)} %get-tuple-element.9, f32[24,137,128]{2,1,0:T(8,128)} %convolution_select_fusion.1), kind=kCustom, calls=%fused_computation.6 | custom fusion | flops 420864 | bytes 5050464 | tf_op jit(solution)/shard_map/scatter-add | solution.py:15
  71.5 6.5 %scatter_fusion.7 = f32[72,137,128]{2,1,0:T(8,128)} fusion(f32[72,137,128]{2,1,0:T(8,128)} %scatter_fusion.6, s32[24]{0:T(128)S(1)} %get-tuple-element.8, f32[24,137,128]{2,1,0:T(8,128)S(1)} %convolution_select_fusion), kind=kCustom, calls=%fused_computation.7 | custom fusion | flops 420864 | bytes 5050464 | tf_op jit(solution)/shard_map/scatter-add | solution.py:15
  78.0 2.9 %fusion.33 = (f32[24,137,128]{2,1,0:T(8,128)S(1)}, f32[24,137,128]{2,1,0:T(8,128)S(1)}, f32[24,137,128]{2,1,0:T(8,128)S(1)}) fusion(f32[72,137,128]{2,1,0:T(8,128)} %scatter_fusion.7), kind=kLoop, calls=%fused_computation.68 | loop fusion | bytes 10100736 | tf_op jit(solution)/shard_map/slice | solution.py:57
  80.9 0.5 copy.56
  81.5 0.0 copy-start.2
  81.5 0.1 collective-permute-start
  81.5 0.5 copy.57
  82.1 3.2 %collective-permute-start.1 = (f32[24,137,128]{2,0,1:T(8,128)S(1)}, f32[24,137,128]{2,0,1:T(8,128)S(1)}, u32[]{:S(2)}, u32[]{:S(2)}) collective-permute-start(f32[24,137,128]{2,0,1:T(8,128)S(1)} %copy.57), channel_id=1, source_target_pairs={{0,1},{1,2},{2,3},{3,4},{4,5},{5,6},{6,7},{7,8},{8,9},{9,10},{10,1... | collective-permute-start | bytes 5050376 | tf_op jit(solution)/shard_map/ppermute | solution.py:10
  85.2 36.7 %collective-permute-done = f32[24,137,128]{2,0,1:T(8,128)S(1)} collective-permute-done((f32[24,137,128]{2,0,1:T(8,128)S(1)}, f32[24,137,128]{2,0,1:T(8,128)S(1)}, u32[]{:S(2)}, u32[]{:S(2)}) %collective-permute-start) | collective-permute-done | bytes 1683488 | tf_op jit(solution)/shard_map/ppermute | solution.py:10
  121.9 0.0 collective-permute-done.1
  122.0 0.0 copy-done.2
  122.0 2.0 %fusion.3 = f32[24,137,128]{2,0,1:T(8,128)} fusion(f32[24,137,128]{2,0,1:T(8,128)S(1)} %collective-permute-done.1, f32[24,137,128]{2,0,1:T(8,128)S(1)} %collective-permute-done, f32[24,137,128]{2,0,1:T(8,128)S(1)} %copy-done.2, f32[24,137,128]{2,1,0:T(8,128)S(1)} %get-tuple-element.5), kind=kLoop, calls=%fused_computation.12 | loop fusion | flops 1262592 | bytes 8417280 | tf_op jit(solution)/shard_map/add | solution.py:58
  (2 shorter events, 0.0 us)
Async XLA Ops:
  0.0 1.5 %copy-start = (bf16[24,137,128]{2,0,1:T(8,128)(2,1)S(1)}, bf16[24,137,128]{2,0,1:T(8,128)(2,1)}, u32[]{:S(2)}) copy-start(bf16[24,137,128]{2,0,1:T(8,128)(2,1)} %param.6) | copy-start | bytes 2525188
  1.5 5.6 %copy-start.1 = (bf16[24,8,128,128]{3,2,1,0:T(8,128)(2,1)S(1)}, bf16[24,8,128,128]{3,2,1,0:T(8,128)(2,1)}, u32[]{:S(2)}) copy-start(bf16[24,8,128,128]{3,2,1,0:T(8,128)(2,1)} %param.8) | copy-start | bytes 18874372
  81.5 40.5 %copy-start.2 = (f32[24,137,128]{2,0,1:T(8,128)S(1)}, f32[24,137,128]{2,0,1:T(8,128)}, u32[]{:S(2)}) copy-start(f32[24,137,128]{2,0,1:T(8,128)} %param.11) | copy-start | bytes 5050372
  81.5 40.5 %collective-permute-start = (f32[24,137,128]{2,0,1:T(8,128)S(1)}, f32[24,137,128]{2,0,1:T(8,128)S(1)}, u32[]{:S(2)}, u32[]{:S(2)}) collective-permute-start(f32[24,137,128]{2,0,1:T(8,128)S(1)} %copy.56), channel_id=1, source_target_pairs={{0,15},{1,0},{2,1},{3,2},{4,3},{5,4},{6,5},{7,6},{8,7},{9,8},{10,9... | collective-permute-start | bytes 5050376 | tf_op jit(solution)/shard_map/ppermute | solution.py:10
  82.1 39.9 %collective-permute-start.1 = (f32[24,137,128]{2,0,1:T(8,128)S(1)}, f32[24,137,128]{2,0,1:T(8,128)S(1)}, u32[]{:S(2)}, u32[]{:S(2)}) collective-permute-start(f32[24,137,128]{2,0,1:T(8,128)S(1)} %copy.57), channel_id=1, source_target_pairs={{0,1},{1,2},{2,3},{3,4},{4,5},{5,6},{6,7},{7,8},{8,9},{9,10},{10,1... | collective-permute-start | bytes 5050376 | tf_op jit(solution)/shard_map/ppermute | solution.py:10
where the time goes:
time: 125 us; the launch traced here: 124 us
  other arithmetic  59.9 us (48%)
  waiting for transfers between devices  36.7 us (29%)
  matrix products  17.3 us (14%)
  local copies, waits for them, and re-layouts  6.66 us (5%)
  starting transfers between devices  3.22 us (3%)
    scatter-add x8, other arithmetic, deposit(): return running.at[slot_column].add(masked)  56.5 us
    ppermute x2, waiting for transfers between devices, from_behind(): return lax.ppermute(value, axis, pairs)  36.7 us
    dot_general x8, matrix products, one_entry(): jnp.einsum('tlb,tbc->tlc', lifted, tile_column, preferred_element_type=jn...  14.7 us
    ppermute x2, starting transfers between devices, from_behind(): return lax.ppermute(value, axis, pairs)  3.22 us
    slice x1, local copies, waits for them, and re-layouts, local(): middle = running[blocks_here:2 * blocks_here]  2.88 us
    broadcast_in_dim x1, local copies, waits for them, and re-layouts, local(): empty = jnp.zeros((3 * blocks_here,) + adjoint_in.shape[1:], jnp.float32)  2.66 us
    dot_general x1, matrix products, local(): jnp.einsum('tml,tmb->tlb', vertical, adjoint_in, preferred_element_type=j...  2.6 us
  transfers between devices with their start and end apart: 2, of which 1 were waited for; matrix products, arithmetic and copies ran while one was open for 0% of the time, Pallas kernels for 0%

commit v1 on v0

v1 whole, which is shorter than its diff:
```python
import functools

import jax
import jax.numpy as jnp
from jax import lax
from jax.experimental import pallas as pl
from jax.experimental.pallas import tpu as pltpu
from jax.sharding import PartitionSpec as P

GROUP = 8
VMEM_BYTES = 48 << 20


def relative(source, first, blocks, everywhere):
    rel = source - first
    rel = jnp.where(rel < -blocks, rel + everywhere, rel)
    return jnp.where(rel >= 2 * blocks, rel - everywhere, rel)


def make_list(pick, trash, axis, src_ref, len_ref, entry_list, slot_list):
    blocks, listed = src_ref.shape
    everywhere = lax.axis_size(axis) * blocks
    first = lax.axis_index(axis) * blocks

    def visit(t, count):
        length = len_ref[t]
        for k in range(listed):
            rel = relative(src_ref[t, k], first, blocks, everywhere)
            keep, slot = pick(rel)
            keep = jnp.logical_and(keep, k < length)
            entry_list[count] = t * listed + k
            slot_list[count] = slot
            count = count + keep.astype(jnp.int32)
        return count

    count = lax.fori_loop(0, blocks, visit, jnp.int32(0))
    for extra in range(GROUP):
        entry_list[count + extra] = 0
        slot_list[count + extra] = trash
    return count


def add_products(count, listed, entry_list, slot_list, lifted, tiles, running):
    def group(g, carry):
        for u in range(GROUP):
            entry = entry_list[g * GROUP + u]
            slot = slot_list[g * GROUP + u]
            product = jnp.dot(
                lifted[lax.div(entry, listed)], tiles[entry], preferred_element_type=jnp.float32
            )
            running[slot] += product
        return carry

    lax.fori_loop(0, lax.div(count + (GROUP - 1), GROUP), group, 0)


def fetch_tiles(tiles_hbm, tiles, sems, parts):
    each = tiles.shape[0] // parts
    copies = []
    for part in range(parts):
        rows = pl.ds(part * each, each)
        copies.append(pltpu.make_async_copy(tiles_hbm.at[rows], tiles.at[rows], sems.at[part]))
    return copies


def pick_rim(blocks, low, up, rel):
    low_from, low_to = low
    up_from, up_to = up
    is_low = jnp.logical_and(rel >= low_from - blocks, rel < low_to - blocks)
    is_up = jnp.logical_and(rel >= up_from + blocks, rel < up_to + blocks)
    slot = jnp.where(is_low, rel + (blocks - low_from), rel - (blocks + up_from) + (low_to - low_from))
    return jnp.logical_or(is_low, is_up), slot


def emit_rims(low_count, up_count, running, low_ref, up_ref):
    def low_body(j, carry):
        low_ref[j] = running[j].astype(low_ref.dtype)
        return carry

    def up_body(j, carry):
        up_ref[j] = running[low_count + j].astype(up_ref.dtype)
        return carry

    lax.fori_loop(0, low_count, low_body, 0)
    lax.fori_loop(0, up_count, up_body, 0)


def clear(running):
    def body(j, carry):
        running[j] = jnp.zeros_like(running[j])
        return carry

    lax.fori_loop(0, running.shape[0], body, 0)


def early_kernel(axis, low, up, parts, src_ref, len_ref, a_hbm, v_hbm, tiles_hbm, low_ref, up_ref, lifted,
                 a, v, tiles, running, entry_list, slot_list, sems, tile_sems):
    blocks, listed = src_ref.shape
    copy_a = pltpu.make_async_copy(a_hbm, a, sems.at[0])
    copy_v = pltpu.make_async_copy(v_hbm, v, sems.at[1])
    copy_v.start()
    copy_a.start()
    copies = fetch_tiles(tiles_hbm, tiles, tile_sems, parts)
    for copy in copies:
        copy.start()
    trash = running.shape[0] - 1
    count = make_list(functools.partial(pick_rim, blocks, low, up), trash, axis, src_ref, len_ref, entry_list, slot_list)
    clear(running)
    copy_v.wait()
    copy_a.wait()

    def lift(i, carry):
        for u in range(4):
            t = i * 4 + u
            lifted[t] = lax.dot_general(
                v[t], a[t], (((0,), (0,)), ((), ())), preferred_element_type=jnp.float32
            ).astype(lifted.dtype)
        return carry

    lax.fori_loop(0, blocks // 4, lift, 0)
    for copy in copies:
        copy.wait()
    add_products(count, listed, entry_list, slot_list, lifted, tiles, running)
    emit_rims(low[1] - low[0], up[1] - up[0], running, low_ref, up_ref)


def late_kernel(axis, low, up, parts, src_ref, len_ref, lifted, tiles_hbm, low_ref, up_ref,
                tiles, running, entry_list, slot_list, tile_sems):
    blocks, listed = src_ref.shape
    copies = fetch_tiles(tiles_hbm, tiles, tile_sems, parts)
    for copy in copies:
        copy.start()
    trash = running.shape[0] - 1
    count = make_list(functools.partial(pick_rim, blocks, low, up), trash, axis, src_ref, len_ref, entry_list, slot_list)
    clear(running)
    for copy in copies:
        copy.wait()
    add_products(count, listed, entry_list, slot_list, lifted, tiles, running)
    emit_rims(low[1] - low[0], up[1] - up[0], running, low_ref, up_ref)


def middle_kernel(axis, parts, low_from, up_from, src_ref, len_ref, lifted, tiles_hbm, prior_hbm, low_hbm, up_hbm, out_hbm,
                  tiles, running, low_got, up_got, entry_list, slot_list, sems, tile_sems):
    blocks, listed = src_ref.shape
    kept = running.at[pl.ds(0, blocks)]
    copy_prior = pltpu.make_async_copy(prior_hbm, kept, sems.at[0])
    copy_low = pltpu.make_async_copy(low_hbm, low_got, sems.at[1])
    copy_up = pltpu.make_async_copy(up_hbm, up_got, sems.at[2])
    copy_prior.start()
    copy_low.start()
    copy_up.start()
    copies = fetch_tiles(tiles_hbm, tiles, tile_sems, parts)
    for copy in copies:
        copy.start()

    def pick(rel):
        return jnp.logical_and(rel >= 0, rel < blocks), rel

    running[blocks] = jnp.zeros_like(running[blocks])
    count = make_list(pick, blocks, axis, src_ref, len_ref, entry_list, slot_list)
    copy_prior.wait()
    copy_low.wait()
    copy_up.wait()

    def add_low(j, carry):
        running[low_from + j] += low_got[j].astype(jnp.float32)
        return carry

    def add_up(j, carry):
        running[up_from + j] += up_got[j].astype(jnp.float32)
        return carry

    lax.fori_loop(0, low_got.shape[0], add_low, 0)
    lax.fori_loop(0, up_got.shape[0], add_up, 0)
    for copy in copies:
        copy.wait()
    add_products(count, listed, entry_list, slot_list, lifted, tiles, running)
    copy_out = pltpu.make_async_copy(kept, out_hbm, sems.at[3])
    copy_out.start()
    copy_out.wait()


SMEM = pl.BlockSpec(memory_space=pltpu.SMEM)
VMEM = pl.BlockSpec(memory_space=pltpu.VMEM)
HBM = pl.BlockSpec(memory_space=pl.ANY)


def shift(value, axis, steps):
    count = lax.axis_size(axis)
    return lax.ppermute(value, axis, [(i, (i + steps) % count) for i in range(count)])


def local(adjoint_in, vertical, tiles, sources, lengths, prior):
    blocks, levels, width = adjoint_in.shape
    listed = tiles.shape[1]
    half = blocks // 2
    parts = 4
    flat = tiles.reshape((blocks * listed,) + tiles.shape[2:])
    rim = jax.ShapeDtypeStruct((half, levels, width), jnp.bfloat16)
    tile_scratch = pltpu.VMEM(flat.shape, flat.dtype)
    rim_running = pltpu.VMEM((blocks + 1, levels, width), jnp.float32)
    lists = [pltpu.SMEM((blocks * listed + GROUP,), jnp.int32)] * 2
    params = pltpu.CompilerParams(vmem_limit_bytes=VMEM_BYTES)
    cost = pl.CostEstimate(flops=400_000_000, bytes_accessed=8_000_000, transcendentals=0)

    low_a, up_a, lifted = pl.pallas_call(
        functools.partial(early_kernel, "col", (0, half), (half, blocks), parts),
        out_shape=[rim, rim, jax.ShapeDtypeStruct(adjoint_in.shape, jnp.bfloat16)],
        in_specs=[SMEM, SMEM, HBM, HBM, HBM],
        out_specs=[VMEM, VMEM, VMEM],
        scratch_shapes=[
            pltpu.VMEM(adjoint_in.shape, adjoint_in.dtype),
            pltpu.VMEM(vertical.shape, vertical.dtype),
            tile_scratch,
            rim_running,
            *lists,
            pltpu.SemaphoreType.DMA((2,)),
            pltpu.SemaphoreType.DMA((parts,)),
        ],
        compiler_params=params,
        cost_estimate=cost,
        name="early",
    )(sources, lengths, adjoint_in, vertical, flat)
    got_low_a = shift(low_a, "col", -1)
    got_up_a = shift(up_a, "col", 1)
    low_b, up_b = pl.pallas_call(
        functools.partial(late_kernel, "col", (half, blocks), (0, half), parts),
        out_shape=[rim, rim],
        in_specs=[SMEM, SMEM, VMEM, HBM],
        out_specs=[VMEM, VMEM],
        scratch_shapes=[tile_scratch, rim_running, *lists, pltpu.SemaphoreType.DMA((parts,))],
        compiler_params=params,
        cost_estimate=cost,
        name="late",
    )(sources, lengths, lifted, flat)
    got_low_b = shift(low_b, "col", -1)
    got_up_b = shift(up_b, "col", 1)
    partial = pl.pallas_call(
        functools.partial(middle_kernel, "col", parts, 0, half),
        out_shape=jax.ShapeDtypeStruct(prior.shape, prior.dtype),
        in_specs=[SMEM, SMEM, VMEM, HBM, HBM, HBM, HBM],
        out_specs=HBM,
        scratch_shapes=[
            tile_scratch,
            rim_running,
            pltpu.VMEM(rim.shape, rim.dtype),
            pltpu.VMEM(rim.shape, rim.dtype),
            *lists,
            pltpu.SemaphoreType.DMA((4,)),
            pltpu.SemaphoreType.DMA((parts,)),
        ],
        compiler_params=params,
        cost_estimate=cost,
        name="middle",
    )(sources, lengths, lifted, flat, prior, got_low_a, got_up_a)
    return partial + jnp.concatenate([got_up_b, got_low_b]).astype(jnp.float32)


def solution(mesh):
    placed = (
        P(("grp", "col"), None, None),
        P(("grp", "col"), None, None),
        P(("grp", "col"), None, None, None),
        P(("grp", "col"), None),
        P(("grp", "col")),
        P(("grp", "col"), None, None),
    )
    return jax.shard_map(
        local, mesh=mesh, in_specs=placed, out_specs=P(("grp", "col"), None, None), check_vma=False
    )
```

time: 125 us -> 35.6 us (0.28)
  other arithmetic: 59.9 us -> 0.18 us
  waiting for transfers between devices: 36.7 us -> 7.71 us
  matrix products: 17.3 us -> 0 us
  Pallas kernels: 0 us -> 16.5 us
  starting transfers between devices: 3.22 us -> 5.69 us
  local copies, waits for them, and re-layouts: 6.66 us -> 4.8 us
    scatter-add x8 -> x0, other arithmetic: 56.5 us -> none  [deposit(): return running.at[slot_column].add(masked)]
    ppermute x2 -> x4, waiting for transfers between devices: 36.7 us -> 7.71 us  [shift(): lax.ppermute(value, axis, [(i, (i + steps) % count) for i in range(count)])]
    dot_general x9 -> x0, matrix products: 17.3 us -> none  [the longest x8 14.7 us: one_entry(): jnp.einsum('tlb,tbc->tlc', lifted, tile_column, preferred_element_type=jn...]
    pallas_call x0 -> x3, Pallas kernels: none -> 16.5 us  [the longest x1 5.95 us: local(): pl.pallas_call(functools.partial(middle_kernel, 'col', parts, 0, half), o...]
    slice x3 -> x0, local copies, waits for them, and re-layouts: 3.97 us -> none  [the longest x1 2.88 us: local(): middle = running[blocks_here:2 * blocks_here]]
    unnamed x6 -> x10, local copies, waits for them, and re-layouts: 0.02 us -> 3.11 us
    broadcast_in_dim x2 -> x0, local copies, waits for them, and re-layouts: 2.67 us -> none  [the longest x1 2.66 us: local(): empty = jnp.zeros((3 * blocks_here,) + adjoint_in.shape[1:], jnp.float32)]
    add x2 -> x1, other arithmetic: 2.66 us -> 0.18 us  [local(): return partial + jnp.concatenate([got_up_b, got_low_b]).astype(jnp.float32)]
  transfers between devices with their start and end apart: 2 -> 4, of which waited for: 1 -> 2; matrix products, arithmetic and copies ran while one was open for 0% -> 1% of each run, Pallas kernels for 0% -> 31%
where the time goes in v1:
time: 35.6 us; the launch traced here: 35 us
  Pallas kernels  16.5 us (46%)
  waiting for transfers between devices  7.71 us (22%)
  starting transfers between devices  5.69 us (16%)
  local copies, waits for them, and re-layouts  4.8 us (13%)
    ppermute x4, waiting for transfers between devices, shift(): lax.ppermute(value, axis, [(i, (i + steps) % count) for i in range(count)])  7.71 us
    pallas_call x1, Pallas kernels, local(): pl.pallas_call(functools.partial(middle_kernel, 'col', parts, 0, half), o...  5.95 us
    pallas_call x1, Pallas kernels, local(): pl.pallas_call(functools.partial(early_kernel, 'col', (0, half), (half, b...  5.81 us
    ppermute x4, starting transfers between devices, shift(): lax.ppermute(value, axis, [(i, (i + steps) % count) for i in range(count)])  5.69 us
    pallas_call x1, Pallas kernels, local(): pl.pallas_call(functools.partial(late_kernel, 'col', (half, blocks), (0,...  4.74 us
    unnamed x10, local copies, waits for them, and re-layouts  3.11 us
    add x1, local copies, waits for them, and re-layouts, local(): return partial + jnp.concatenate([got_up_b, got_low_b]).astype(jnp.float32)  1.7 us
  transfers between devices with their start and end apart: 4, of which 2 were waited for; matrix products, arithmetic and copies ran while one was open for 1% of the time, Pallas kernels for 31%

profile of v1, /device:TPU:1, one launch (start us, length us, event | category | flops | bytes accessed | tf_op | source)
XLA Modules:
  0.0 35.0 jit_solution(16400788901584588095)
XLA Ops:
  0.0 0.0 copy-start.2
  0.0 0.8 %copy.10.src_ref = s32[24,8]{1,0:T(8,128)S(1)} copy(s32[24,8]{0,1:T(8,128)} %param.9) | data formatting | bytes 1536 | tf_op args[3]
  0.8 0.0 copy-start
  0.8 1.8 %copy.9.v_hbm = bf16[24,137,137]{2,1,0:T(8,128)(2,1)S(1)} copy(bf16[24,137,137]{2,0,1:T(8,128)(2,1)} %param.7) | data formatting | bytes 1801824 | tf_op args[1]
  2.6 0.0 copy-done.2
  2.7 0.1 copy.8.a_hbm
  2.8 0.0 copy-done
  2.8 5.8 %early.1 = (bf16[12,137,128]{2,1,0:T(8,128)(2,1)S(1)}, bf16[12,137,128]{2,1,0:T(8,128)(2,1)S(1)}, bf16[24,137,128]{2,1,0:T(8,128)(2,1)S(1)}) custom-call(s32[24,8]{1,0:T(8,128)S(1)} %copy.10.src_ref, s32[24]{0:T(128)S(1)} %copy-done, bf16[24,137,128]{2,1,0:T(8,128)(2,1)S(1)} %copy.8.a_hbm, bf16[24,137,137]{2,1,0:T(8,128)(2,1)S(1)} %copy.9.v_hbm, ...), custom_call_target="tpu_custom_call" | custom-call | flops 400000000 | bytes 8000000 | tf_op jit(solution)/shard_map/early/pallas_call | solution.py:206
  8.6 0.1 collective-permute-start
  8.7 2.9 %collective-permute-start.1 = (bf16[12,137,128]{2,1,0:T(8,128)(2,1)S(1)}, bf16[12,137,128]{2,1,0:T(8,128)(2,1)S(1)}, u32[]{:S(2)}, u32[]{:S(2)}) collective-permute-start(bf16[12,137,128]{2,1,0:T(8,128)(2,1)S(1)} %get-tuple-element.12), channel_id=1, source_target_pairs={{0,1},{1,2},{2,3},{3,4},{4,5},{5,6},{6,7},{7,8},{8,9},{9,10},{10,1... | collective-permute-start | bytes 1262600 | tf_op jit(solution)/shard_map/ppermute | solution.py:190
  11.7 0.0 copy-start.1
  11.7 4.7 %late.1 = (bf16[12,137,128]{2,1,0:T(8,128)(2,1)S(1)}, bf16[12,137,128]{2,1,0:T(8,128)(2,1)S(1)}) custom-call(s32[24,8]{1,0:T(8,128)S(1)} %copy.10.src_ref, s32[24]{0:T(128)S(1)} %copy-done, bf16[24,137,128]{2,1,0:T(8,128)(2,1)S(1)} %get-tuple-element.10.lifted, bf16[192,128,128]{2,1,0:T(8,128)(2,1)} %bitcast.2), custom_call_target="tpu_custom_call" | custom-call | flops 400000000 | bytes 8000000 | tf_op jit(solution)/shard_map/late/pallas_call | solution.py:226
  16.4 0.5 %collective-permute-start.2 = (bf16[12,137,128]{2,1,0:T(8,128)(2,1)S(1)}, bf16[12,137,128]{2,1,0:T(8,128)(2,1)S(1)}, u32[]{:S(2)}, u32[]{:S(2)}) collective-permute-start(bf16[12,137,128]{2,1,0:T(8,128)(2,1)S(1)} %get-tuple-element.13), channel_id=1, source_target_pairs={{0,1},{1,2},{2,3},{3,4},{4,5},{5,6},{6,7},{7,8},{8,9},{9,10},{10,1... | collective-permute-start | bytes 1262600 | tf_op jit(solution)/shard_map/ppermute | solution.py:190
  16.9 2.1 %collective-permute-start.3 = (bf16[12,137,128]{2,1,0:T(8,128)(2,1)S(1)}, bf16[12,137,128]{2,1,0:T(8,128)(2,1)S(1)}, u32[]{:S(2)}, u32[]{:S(2)}) collective-permute-start(bf16[12,137,128]{2,1,0:T(8,128)(2,1)S(1)} %get-tuple-element.14), channel_id=1, source_target_pairs={{0,15},{1,0},{2,1},{3,2},{4,3},{5,4},{6,5},{7,6},{8,7},{9,8},{10,9... | collective-permute-start | bytes 1262600 | tf_op jit(solution)/shard_map/ppermute | solution.py:190
  19.0 0.0 copy-done.1
  19.1 0.3 copy.11.prior_hbm
  19.4 0.0 collective-permute-done.low_hbm
  19.4 7.0 %collective-permute-done.1.up_hbm = bf16[12,137,128]{2,1,0:T(8,128)(2,1)S(1)} collective-permute-done((bf16[12,137,128]{2,1,0:T(8,128)(2,1)S(1)}, bf16[12,137,128]{2,1,0:T(8,128)(2,1)S(1)}, u32[]{:S(2)}, u32[]{:S(2)}) %collective-permute-start.1) | collective-permute-done | bytes 420896 | tf_op jit(solution)/shard_map/ppermute | solution.py:190
  26.4 6.0 %middle.1 = f32[24,137,128]{2,1,0:T(8,128)S(1)} custom-call(s32[24,8]{1,0:T(8,128)S(1)} %copy.10.src_ref, s32[24]{0:T(128)S(1)} %copy-done, bf16[24,137,128]{2,1,0:T(8,128)(2,1)S(1)} %get-tuple-element.10.lifted, bf16[192,128,128]{2,1,0:T(8,128)(2,1)} %bitcast.3, f32[24,137,128]{2,1,0:T(8,128)S(1)} %copy.11.prior_hbm, ...), custom_call_target="tpu_custom_call" | custom-call | flops 400000000 | bytes 8000000 | tf_op jit(solution)/shard_map/middle/pallas_call | solution.py:238
  32.4 0.0 collective-permute-done.2
  32.4 0.7 %collective-permute-done.3 = bf16[12,137,128]{2,1,0:T(8,128)(2,1)S(1)} collective-permute-done((bf16[12,137,128]{2,1,0:T(8,128)(2,1)S(1)}, bf16[12,137,128]{2,1,0:T(8,128)(2,1)S(1)}, u32[]{:S(2)}, u32[]{:S(2)}) %collective-permute-start.3) | collective-permute-done | bytes 420896 | tf_op jit(solution)/shard_map/ppermute | solution.py:190
  33.1 0.2 convert_add_fusion
  33.3 1.7 %copy.13 = f32[24,137,128]{2,0,1:T(8,128)} copy(f32[24,137,128]{2,1,0:T(8,128)S(1)} %convert_add_fusion) | data formatting | bytes 3366912 | tf_op jit(solution)/shard_map/add | solution.py:256
Async XLA Ops:
  0.0 2.6 %copy-start.2 = (bf16[24,137,128]{2,0,1:T(8,128)(2,1)S(1)}, bf16[24,137,128]{2,0,1:T(8,128)(2,1)}, u32[]{:S(2)}) copy-start(bf16[24,137,128]{2,0,1:T(8,128)(2,1)} %param.6) | copy-start | bytes 2525188
  0.8 1.9 %copy-start = (s32[24]{0:T(128)S(1)}, s32[24]{0:T(128)}, u32[]{:S(2)}) copy-start(s32[24]{0:T(128)} %len_ref.5) | copy-start | bytes 292
  8.6 10.8 %collective-permute-start = (bf16[12,137,128]{2,1,0:T(8,128)(2,1)S(1)}, bf16[12,137,128]{2,1,0:T(8,128)(2,1)S(1)}, u32[]{:S(2)}, u32[]{:S(2)}) collective-permute-start(bf16[12,137,128]{2,1,0:T(8,128)(2,1)S(1)} %get-tuple-element.11), channel_id=1, source_target_pairs={{0,15},{1,0},{2,1},{3,2},{4,3},{5,4},{6,5},{7,6},{8,7},{9,8},{10,9... | collective-permute-start | bytes 1262600 | tf_op jit(solution)/shard_map/ppermute | solution.py:190
  8.7 17.7 %collective-permute-start.1 = (bf16[12,137,128]{2,1,0:T(8,128)(2,1)S(1)}, bf16[12,137,128]{2,1,0:T(8,128)(2,1)S(1)}, u32[]{:S(2)}, u32[]{:S(2)}) collective-permute-start(bf16[12,137,128]{2,1,0:T(8,128)(2,1)S(1)} %get-tuple-element.12), channel_id=1, source_target_pairs={{0,1},{1,2},{2,3},{3,4},{4,5},{5,6},{6,7},{7,8},{8,9},{9,10},{10,1... | collective-permute-start | bytes 1262600 | tf_op jit(solution)/shard_map/ppermute | solution.py:190
  11.7 7.4 %copy-start.1 = (f32[24,137,128]{2,0,1:T(8,128)S(1)}, f32[24,137,128]{2,0,1:T(8,128)}, u32[]{:S(2)}) copy-start(f32[24,137,128]{2,0,1:T(8,128)} %param.11) | copy-start | bytes 5050372
  16.4 15.9 %collective-permute-start.2 = (bf16[12,137,128]{2,1,0:T(8,128)(2,1)S(1)}, bf16[12,137,128]{2,1,0:T(8,128)(2,1)S(1)}, u32[]{:S(2)}, u32[]{:S(2)}) collective-permute-start(bf16[12,137,128]{2,1,0:T(8,128)(2,1)S(1)} %get-tuple-element.13), channel_id=1, source_target_pairs={{0,1},{1,2},{2,3},{3,4},{4,5},{5,6},{6,7},{7,8},{8,9},{9,10},{10,1... | collective-permute-start | bytes 1262600 | tf_op jit(solution)/shard_map/ppermute | solution.py:190
  16.9 16.2 %collective-permute-start.3 = (bf16[12,137,128]{2,1,0:T(8,128)(2,1)S(1)}, bf16[12,137,128]{2,1,0:T(8,128)(2,1)S(1)}, u32[]{:S(2)}, u32[]{:S(2)}) collective-permute-start(bf16[12,137,128]{2,1,0:T(8,128)(2,1)S(1)} %get-tuple-element.14), channel_id=1, source_target_pairs={{0,15},{1,0},{2,1},{3,2},{4,3},{5,4},{6,5},{7,6},{8,7},{9,8},{10,9... | collective-permute-start | bytes 1262600 | tf_op jit(solution)/shard_map/ppermute | solution.py:190

commit v2 on v0

v2 whole, which is shorter than its diff:
```python
import functools

import jax
import jax.numpy as jnp
from jax import lax
from jax.experimental import pallas as pl
from jax.experimental.pallas import tpu as pltpu
from jax.sharding import PartitionSpec as P

GROUP = 8
UNROLL = 4
FIRST = 16
VMEM_BYTES = 48 << 20


def relative(source, first, blocks, everywhere):
    rel = source - first
    rel = jnp.where(rel < -blocks, rel + everywhere, rel)
    return jnp.where(rel >= 2 * blocks, rel - everywhere, rel)


def list_entries(t, count, pick, first, everywhere, src_ref, len_ref, entry_list, row_list):
    listed, blocks = src_ref.shape
    length = len_ref[t]
    for k in range(listed):
        rel = relative(src_ref[k, t], first, blocks, everywhere)
        keep, row = pick(rel)
        keep = jnp.logical_and(keep, k < length)
        entry_list[count] = t * listed + k
        row_list[count] = row
        count = count + keep.astype(jnp.int32)
    return count


def close_list(count, zero_tile, entry_list, row_list, tiles):
    for extra in range(GROUP):
        entry_list[count + extra] = zero_tile
        row_list[count + extra] = 0
    tiles[zero_tile] = jnp.zeros_like(tiles[zero_tile])


def add_products(count, listed, width, entry_list, row_list, lifted, tiles, running):
    last = lifted.shape[0] - 1
    levels = lifted.shape[1]

    def group(g, carry):
        for u in range(GROUP):
            entry = entry_list[g * GROUP + u]
            row = row_list[g * GROUP + u]
            t = jnp.minimum(lax.div(entry, listed), last)
            product = jnp.dot(lifted[t], tiles[entry], preferred_element_type=jnp.float32)
            rows = pl.ds(row, levels, stride=width)
            running[rows, :] = running[rows, :] + product
        return carry

    lax.fori_loop(0, lax.div(count + (GROUP - 1), GROUP), group, 0)


def fetch_tiles(tiles_hbm, tiles, sems, parts):
    each = tiles_hbm.shape[0] // parts
    copies = []
    for part in range(parts):
        rows = pl.ds(part * each, each)
        copies.append(pltpu.make_async_copy(tiles_hbm.at[rows], tiles.at[rows], sems.at[part]))
    return copies


def pick_rim(blocks, low_from, up_from, width, up_base, rel):
    low = rel + (blocks - low_from)
    up = rel - (blocks + up_from)
    is_low = jnp.logical_and(low >= 0, low < width)
    is_up = jnp.logical_and(up >= 0, up < width)
    return jnp.logical_or(is_low, is_up), jnp.where(is_low, low, up + up_base)


def here(axis, blocks):
    return lax.axis_index(axis) * blocks, lax.axis_size(axis) * blocks


def emit(running, up_base, low_ref, up_ref):
    rows = low_ref.shape[0]
    low_ref[...] = running[:rows].astype(low_ref.dtype)
    up_ref[...] = running[up_base : up_base + rows].astype(up_ref.dtype)


def early_kernel(axis, low_from, up_from, width, parts, src_ref, len_ref, a, v, tiles_hbm, low_ref, up_ref, lifted,
                 tiles, running, entry_list, row_list, tile_sems):
    listed, blocks = src_ref.shape
    up_base = running.shape[0] // 2
    first, everywhere = here(axis, blocks)
    copies = fetch_tiles(tiles_hbm, tiles, tile_sems, parts)
    for copy in copies:
        copy.start()
    running[...] = jnp.zeros_like(running)
    pick = functools.partial(pick_rim, blocks, low_from, up_from, width, up_base)

    def lift(i, count):
        for u in range(UNROLL):
            t = i * UNROLL + u
            lifted[t] = lax.dot_general(
                v[t], a[t], (((0,), (0,)), ((), ())), preferred_element_type=jnp.float32
            ).astype(lifted.dtype)
            count = list_entries(t, count, pick, first, everywhere, src_ref, len_ref, entry_list, row_list)
        return count

    count = lax.fori_loop(0, blocks // UNROLL, lift, jnp.int32(0))
    close_list(count, blocks * listed, entry_list, row_list, tiles)
    for copy in copies:
        copy.wait()
    add_products(count, listed, width, entry_list, row_list, lifted, tiles, running)
    emit(running, up_base, low_ref, up_ref)


def late_kernel(axis, low_from, up_from, width, parts, src_ref, len_ref, lifted, tiles_hbm, low_ref, up_ref,
                tiles, running, entry_list, row_list, tile_sems):
    listed, blocks = src_ref.shape
    up_base = running.shape[0] // 2
    first, everywhere = here(axis, blocks)
    copies = fetch_tiles(tiles_hbm, tiles, tile_sems, parts)
    for copy in copies:
        copy.start()
    running[...] = jnp.zeros_like(running)
    pick = functools.partial(pick_rim, blocks, low_from, up_from, width, up_base)
    visit = lambda t, count: list_entries(t, count, pick, first, everywhere, src_ref, len_ref, entry_list, row_list)
    count = lax.fori_loop(0, blocks, visit, jnp.int32(0))
    close_list(count, blocks * listed, entry_list, row_list, tiles)
    for copy in copies:
        copy.wait()
    add_products(count, listed, width, entry_list, row_list, lifted, tiles, running)
    emit(running, up_base, low_ref, up_ref)


def middle_kernel(axis, parts, src_ref, len_ref, lifted, tiles_hbm, prior_hbm, running,
                  tiles, entry_list, row_list, prior_sem, tile_sems):
    listed, blocks = src_ref.shape
    first, everywhere = here(axis, blocks)
    copy_prior = pltpu.make_async_copy(prior_hbm, running, prior_sem)
    copy_prior.start()
    copies = fetch_tiles(tiles_hbm, tiles, tile_sems, parts)
    for copy in copies:
        copy.start()

    def pick(rel):
        return jnp.logical_and(rel >= 0, rel < blocks), rel

    visit = lambda t, count: list_entries(t, count, pick, first, everywhere, src_ref, len_ref, entry_list, row_list)
    count = lax.fori_loop(0, blocks, visit, jnp.int32(0))
    close_list(count, blocks * listed, entry_list, row_list, tiles)
    copy_prior.wait()
    for copy in copies:
        copy.wait()
    add_products(count, listed, blocks, entry_list, row_list, lifted, tiles, running)


SMEM = pl.BlockSpec(memory_space=pltpu.SMEM)
VMEM = pl.BlockSpec(memory_space=pltpu.VMEM)
HBM = pl.BlockSpec(memory_space=pl.ANY)


def shift(value, axis, steps):
    count = lax.axis_size(axis)
    return lax.ppermute(value, axis, [(i, (i + steps) % count) for i in range(count)])


def local(adjoint_in, vertical, tiles, sources, lengths, prior):
    blocks, levels, width = adjoint_in.shape
    listed = tiles.shape[1]
    wide = min(blocks, FIRST)
    thin = blocks - wide
    parts = 4
    flat = tiles.reshape((blocks * listed,) + tiles.shape[2:])
    by_entry = sources.T
    prior_rows = prior.transpose(1, 0, 2).reshape(levels * blocks, width)
    tile_scratch = pltpu.VMEM((blocks * listed + 1,) + flat.shape[1:], flat.dtype)
    lists = [pltpu.SMEM((blocks * listed + GROUP,), jnp.int32)] * 2
    params = pltpu.CompilerParams(vmem_limit_bytes=VMEM_BYTES)
    cost = pl.CostEstimate(flops=400_000_000, bytes_accessed=8_000_000, transcendentals=0)

    def rim(count):
        return jax.ShapeDtypeStruct((levels * count, width), jnp.bfloat16)

    def rim_running(count):
        return pltpu.VMEM((2 * (-(-levels * count // 16) * 16), width), jnp.float32)

    low_a, up_a, lifted = pl.pallas_call(
        functools.partial(early_kernel, "col", 0, thin, wide, parts),
        out_shape=[rim(wide), rim(wide), jax.ShapeDtypeStruct(adjoint_in.shape, jnp.bfloat16)],
        in_specs=[SMEM, SMEM, VMEM, VMEM, HBM],
        out_specs=[VMEM, VMEM, VMEM],
        scratch_shapes=[tile_scratch, rim_running(wide), *lists, pltpu.SemaphoreType.DMA((parts,))],
        compiler_params=params,
        cost_estimate=cost,
        name="early",
    )(by_entry, lengths, adjoint_in, vertical, flat)
    low_a = shift(low_a, "col", -1)
    up_a = shift(up_a, "col", 1)
    low_b, up_b = pl.pallas_call(
        functools.partial(late_kernel, "col", wide, 0, thin, parts),
        out_shape=[rim(thin), rim(thin)],
        in_specs=[SMEM, SMEM, VMEM, HBM],
        out_specs=[VMEM, VMEM],
        scratch_shapes=[tile_scratch, rim_running(thin), *lists, pltpu.SemaphoreType.DMA((parts,))],
        compiler_params=params,
        cost_estimate=cost,
        name="late",
    )(by_entry, lengths, lifted, flat)
    low_b = shift(low_b, "col", -1)
    up_b = shift(up_b, "col", 1)
    middle = pl.pallas_call(
        functools.partial(middle_kernel, "col", parts),
        out_shape=jax.ShapeDtypeStruct(prior_rows.shape, prior.dtype),
        in_specs=[SMEM, SMEM, VMEM, HBM, HBM],
        out_specs=VMEM,
        scratch_shapes=[tile_scratch, *lists, pltpu.SemaphoreType.DMA, pltpu.SemaphoreType.DMA((parts,))],
        compiler_params=params,
        cost_estimate=cost,
        name="middle",
    )(by_entry, lengths, lifted, flat, prior_rows)

    def joined(left, right):
        pieces = [piece.reshape(levels, -1, width) for piece in (left, right)]
        return jnp.concatenate(pieces, axis=1).astype(jnp.float32)

    total = middle.reshape(levels, blocks, width) + joined(low_a, low_b) + joined(up_b, up_a)
    return total.transpose(1, 0, 2)


def solution(mesh):
    placed = (
        P(("grp", "col"), None, None),
        P(("grp", "col"), None, None),
        P(("grp", "col"), None, None, None),
        P(("grp", "col"), None),
        P(("grp", "col")),
        P(("grp", "col"), None, None),
    )
    return jax.shard_map(
        local, mesh=mesh, in_specs=placed, out_specs=P(("grp", "col"), None, None), check_vma=False
    )
```

time: 125 us -> 33.6 us (0.27)
  the two profiles are of different devices: /device:TPU:1 before, /device:TPU:0 now
where the time goes in v2:
time: 33.6 us; the launch traced here: 33.9 us
  Pallas kernels  16.3 us (49%)
  starting transfers between devices  10.9 us (32%)
  waiting for transfers between devices  2.71 us (8%)
  local copies, waits for them, and re-layouts  2.38 us (7%)
  other arithmetic  1.5 us (4%)
    ppermute x4, starting transfers between devices, shift(): lax.ppermute(value, axis, [(i, (i + steps) % count) for i in range(count)])  10.9 us
    pallas_call x1, Pallas kernels, local(): pl.pallas_call(functools.partial(middle_kernel, 'col', parts), out_shape=...  5.97 us
    pallas_call x1, Pallas kernels, local(): pl.pallas_call(functools.partial(early_kernel, 'col', 0, thin, wide, part...  5.66 us
    pallas_call x1, Pallas kernels, local(): pl.pallas_call(functools.partial(late_kernel, 'col', wide, 0, thin, parts...  4.64 us
    ppermute x4, waiting for transfers between devices, shift(): lax.ppermute(value, axis, [(i, (i + steps) % count) for i in range(count)])  2.71 us
    unnamed x10, local copies, waits for them, and re-layouts  2.38 us
    transpose x1, other arithmetic, local(): return total.transpose(1, 0, 2)  1.5 us
  transfers between devices with their start and end apart: 4, of which 1 were waited for; matrix products, arithmetic and copies ran while one was open for 0% of the time, Pallas kernels for 31%

profile of v2, /device:TPU:0, one launch (start us, length us, event | category | flops | bytes accessed | tf_op | source)
XLA Modules:
  0.0 33.9 jit_solution(5549147912231962316)
XLA Ops:
  0.0 0.0 copy-start.3
  0.0 1.4 %copy.7.a = bf16[24,137,128]{2,1,0:T(8,128)(2,1)S(1)} copy(bf16[24,137,128]{2,0,1:T(8,128)(2,1)} %param.6) | data formatting | bytes 1683456 | tf_op args[0]
  1.4 0.3 copy-done.3
  1.7 0.0 copy-start.1
  1.7 0.0 copy-start.2
  1.7 0.3 %copy.8.v = bf16[24,137,137]{2,1,0:T(8,128)(2,1)S(1)} copy(bf16[24,137,137]{2,0,1:T(8,128)(2,1)S(1)} %copy-done.3) | data formatting | bytes 1801824 | tf_op args[1]
  2.1 0.3 copy-done.1
  2.4 0.0 copy-done.2
  2.4 5.7 %early.1 = (bf16[2192,128]{1,0:T(8,128)(2,1)S(1)}, bf16[2192,128]{1,0:T(8,128)(2,1)S(1)}, bf16[24,137,128]{2,1,0:T(8,128)(2,1)S(1)}) custom-call(s32[8,24]{1,0:T(8,128)S(1)} %bitcast.14, s32[24]{0:T(128)S(1)} %copy-done.2, bf16[24,137,128]{2,1,0:T(8,128)(2,1)S(1)} %copy.7.a, bf16[24,137,137]{2,1,0:T(8,128)(2,1)S(1)} %copy.8.v, bf16[192,128,128]{2,1,0:T(8,128)(2,1)} %bitcast.17), custom_call_target="tpu_custom_call" | custom-call | flops 400000000 | bytes 8000000 | tf_op jit(solution)/shard_map/early/pallas_call | solution.py:185
  8.1 6.1 %collective-permute-start = (bf16[2192,128]{1,0:T(8,128)(2,1)S(1)}, bf16[2192,128]{1,0:T(8,128)(2,1)S(1)}, u32[]{:S(2)}, u32[]{:S(2)}) collective-permute-start(bf16[2192,128]{1,0:T(8,128)(2,1)S(1)} %get-tuple-element.11), channel_id=1, source_target_pairs={{0,15},{1,0},{2,1},{3,2},{4,3},{5,4},{6,5},{7,6},{8,7},{9,8},{10,9... | collective-permute-start | bytes 1683464 | tf_op jit(solution)/shard_map/ppermute | solution.py:162
  14.1 0.0 collective-permute-start.3
  14.1 0.0 copy-start
  14.1 4.6 %late.1 = (bf16[1096,128]{1,0:T(8,128)(2,1)S(1)}, bf16[1096,128]{1,0:T(8,128)(2,1)S(1)}) custom-call(s32[8,24]{1,0:T(8,128)S(1)} %bitcast.15, s32[24]{0:T(128)S(1)} %copy-done.2, bf16[24,137,128]{2,1,0:T(8,128)(2,1)S(1)} %get-tuple-element.10.lifted, bf16[192,128,128]{2,1,0:T(8,128)(2,1)} %bitcast.18), custom_call_target="tpu_custom_call" | custom-call | flops 400000000 | bytes 8000000 | tf_op jit(solution)/shard_map/late/pallas_call | solution.py:197
  18.8 4.9 %collective-permute-start.1 = (bf16[1096,128]{1,0:T(8,128)(2,1)S(1)}, bf16[1096,128]{1,0:T(8,128)(2,1)S(1)}, u32[]{:S(2)}, u32[]{:S(2)}) collective-permute-start(bf16[1096,128]{1,0:T(8,128)(2,1)S(1)} %get-tuple-element.12), channel_id=1, source_target_pairs={{0,15},{1,0},{2,1},{3,2},{4,3},{5,4},{6,5},{7,6},{8,7},{9,8},{10,9... | collective-permute-start | bytes 841736 | tf_op jit(solution)/shard_map/ppermute | solution.py:162
  23.7 0.0 collective-permute-start.2
  23.7 0.0 copy-done
  23.7 6.0 %middle.1 = f32[3288,128]{1,0:T(8,128)S(1)} custom-call(s32[8,24]{1,0:T(8,128)S(1)} %bitcast.16, s32[24]{0:T(128)S(1)} %copy-done.2, bf16[24,137,128]{2,1,0:T(8,128)(2,1)S(1)} %get-tuple-element.10.lifted, bf16[192,128,128]{2,1,0:T(8,128)(2,1)} %bitcast.19, f32[3288,128]{1,0:T(8,128)S(1)} %bitcast.13), custom_call_target="tpu_custom_call" | custom-call | flops 400000000 | bytes 8000000 | tf_op jit(solution)/shard_map/middle/pallas_call | solution.py:209
  29.6 0.0 collective-permute-done.1
  29.6 2.7 %collective-permute-done.2 = bf16[1096,128]{1,0:T(8,128)(2,1)S(1)} collective-permute-done((bf16[1096,128]{1,0:T(8,128)(2,1)S(1)}, bf16[1096,128]{1,0:T(8,128)(2,1)S(1)}, u32[]{:S(2)}, u32[]{:S(2)}) %collective-permute-start.2) | collective-permute-done | bytes 280608 | tf_op jit(solution)/shard_map/ppermute | solution.py:162
  32.3 0.0 collective-permute-done
  32.3 0.0 collective-permute-done.3
  32.4 1.5 %add_bitcast_fusion = f32[24,137,128]{2,0,1:T(8,128)} fusion(f32[137,24,128]{2,1,0:T(8,128)S(1)} %bitcast.12, bf16[137,8,128]{2,1,0:T(8,128)(2,1)S(1)} %bitcast.22, bf16[137,16,128]{2,1,0:T(8,128)(2,1)S(1)} %bitcast.20, bf16[137,16,128]{2,1,0:T(8,128)(2,1)S(1)} %bitcast.21, bf16[137,8,128]{2,1,0:T(8,128)(2,1)S(1)} %bitcast.23), kind=kLoop, calls=%fused_computation | loop fusion | flops 4208640 | bytes 5050368 | tf_op jit(solution)/shard_map/transpose | solution.py:225
Async XLA Ops:
  0.0 1.7 %copy-start.3 = (bf16[24,137,137]{2,0,1:T(8,128)(2,1)S(1)}, bf16[24,137,137]{2,0,1:T(8,128)(2,1)}, u32[]{:S(2)}) copy-start(bf16[24,137,137]{2,0,1:T(8,128)(2,1)} %param.7) | copy-start | bytes 2702740
  1.7 0.7 %copy-start.1 = (s32[24,8]{0,1:T(8,128)S(1)}, s32[24,8]{0,1:T(8,128)}, u32[]{:S(2)}) copy-start(s32[24,8]{0,1:T(8,128)} %param.9) | copy-start | bytes 2308
  1.7 0.7 %copy-start.2 = (s32[24]{0:T(128)S(1)}, s32[24]{0:T(128)}, u32[]{:S(2)}) copy-start(s32[24]{0:T(128)} %len_ref.5) | copy-start | bytes 292
  8.1 24.3 %collective-permute-start = (bf16[2192,128]{1,0:T(8,128)(2,1)S(1)}, bf16[2192,128]{1,0:T(8,128)(2,1)S(1)}, u32[]{:S(2)}, u32[]{:S(2)}) collective-permute-start(bf16[2192,128]{1,0:T(8,128)(2,1)S(1)} %get-tuple-element.11), channel_id=1, source_target_pairs={{0,15},{1,0},{2,1},{3,2},{4,3},{5,4},{6,5},{7,6},{8,7},{9,8},{10,9... | collective-permute-start | bytes 1683464 | tf_op jit(solution)/shard_map/ppermute | solution.py:162
  14.1 18.2 %collective-permute-start.3 = (bf16[2192,128]{1,0:T(8,128)(2,1)S(1)}, bf16[2192,128]{1,0:T(8,128)(2,1)S(1)}, u32[]{:S(2)}, u32[]{:S(2)}) collective-permute-start(bf16[2192,128]{1,0:T(8,128)(2,1)S(1)} %get-tuple-element.14), channel_id=1, source_target_pairs={{0,1},{1,2},{2,3},{3,4},{4,5},{5,6},{6,7},{7,8},{8,9},{9,10},{10,1... | collective-permute-start | bytes 1683464 | tf_op jit(solution)/shard_map/ppermute | solution.py:162
  14.1 9.5 %copy-start = (f32[24,137,128]{2,0,1:T(8,128)S(1)}, f32[24,137,128]{2,0,1:T(8,128)}, u32[]{:S(2)}) copy-start(f32[24,137,128]{2,0,1:T(8,128)} %param.11) | copy-start | bytes 5050372
  18.8 10.9 %collective-permute-start.1 = (bf16[1096,128]{1,0:T(8,128)(2,1)S(1)}, bf16[1096,128]{1,0:T(8,128)(2,1)S(1)}, u32[]{:S(2)}, u32[]{:S(2)}) collective-permute-start(bf16[1096,128]{1,0:T(8,128)(2,1)S(1)} %get-tuple-element.12), channel_id=1, source_target_pairs={{0,15},{1,0},{2,1},{3,2},{4,3},{5,4},{6,5},{7,6},{8,7},{9,8},{10,9... | collective-permute-start | bytes 841736 | tf_op jit(solution)/shard_map/ppermute | solution.py:162
  23.7 8.7 %collective-permute-start.2 = (bf16[1096,128]{1,0:T(8,128)(2,1)S(1)}, bf16[1096,128]{1,0:T(8,128)(2,1)S(1)}, u32[]{:S(2)}, u32[]{:S(2)}) collective-permute-start(bf16[1096,128]{1,0:T(8,128)(2,1)S(1)} %get-tuple-element.13), channel_id=1, source_target_pairs={{0,1},{1,2},{2,3},{3,4},{4,5},{5,6},{6,7},{7,8},{8,9},{9,10},{10,1... | collective-permute-start | bytes 841736 | tf_op jit(solution)/shard_map/ppermute | solution.py:162

commit v3 on v2

--- a/solution.py
+++ b/solution.py
@@ -39,7 +39,7 @@
     tiles[zero_tile] = jnp.zeros_like(tiles[zero_tile])
 
 
-def add_products(count, listed, width, entry_list, row_list, lifted, tiles, running):
+def add_products(count, listed, stride, entry_list, row_list, lifted, tiles, running):
     last = lifted.shape[0] - 1
     levels = lifted.shape[1]
 
@@ -49,7 +49,7 @@
             row = row_list[g * GROUP + u]
             t = jnp.minimum(lax.div(entry, listed), last)
             product = jnp.dot(lifted[t], tiles[entry], preferred_element_type=jnp.float32)
-            rows = pl.ds(row, levels, stride=width)
+            rows = pl.ds(row, levels, stride=stride)
             running[rows, :] = running[rows, :] + product
         return carry
 
@@ -77,13 +77,15 @@
     return lax.axis_index(axis) * blocks, lax.axis_size(axis) * blocks
 
 
-def emit(running, up_base, low_ref, up_ref):
-    rows = low_ref.shape[0]
-    low_ref[...] = running[:rows].astype(low_ref.dtype)
-    up_ref[...] = running[up_base : up_base + rows].astype(up_ref.dtype)
-
-
-def early_kernel(axis, low_from, up_from, width, parts, src_ref, len_ref, a, v, tiles_hbm, low_ref, up_ref, lifted,
+def emit(running, up_base, stride, width, low_ref, up_ref):
+    lanes = running.shape[1]
+    for base, ref in ((0, low_ref), (up_base, up_ref)):
+        levels = ref.shape[0] // width
+        rows = running[base : base + levels * stride].reshape(levels, stride, lanes)
+        ref[...] = rows[:, :width].reshape(levels * width, lanes).astype(ref.dtype)
+
+
+def early_kernel(axis, low_from, up_from, width, stride, parts, src_ref, len_ref, a, v, tiles_hbm, low_ref, up_ref, lifted,
                  tiles, running, entry_list, row_list, tile_sems):
     listed, blocks = src_ref.shape
     up_base = running.shape[0] // 2
@@ -107,11 +109,11 @@
     close_list(count, blocks * listed, entry_list, row_list, tiles)
     for copy in copies:
         copy.wait()
-    add_products(count, listed, width, entry_list, row_list, lifted, tiles, running)
-    emit(running, up_base, low_ref, up_ref)
-
-
-def late_kernel(axis, low_from, up_from, width, parts, src_ref, len_ref, lifted, tiles_hbm, low_ref, up_ref,
+    add_products(count, listed, stride, entry_list, row_list, lifted, tiles, running)
+    emit(running, up_base, stride, width, low_ref, up_ref)
+
+
+def late_kernel(axis, low_from, up_from, width, stride, parts, src_ref, len_ref, lifted, tiles_hbm, low_ref, up_ref,
                 tiles, running, entry_list, row_list, tile_sems):
     listed, blocks = src_ref.shape
     up_base = running.shape[0] // 2
@@ -126,8 +128,8 @@
     close_list(count, blocks * listed, entry_list, row_list, tiles)
     for copy in copies:
         copy.wait()
-    add_products(count, listed, width, entry_list, row_list, lifted, tiles, running)
-    emit(running, up_base, low_ref, up_ref)
+    add_products(count, listed, stride, entry_list, row_list, lifted, tiles, running)
+    emit(running, up_base, stride, width, low_ref, up_ref)
 
 
 def middle_kernel(axis, parts, src_ref, len_ref, lifted, tiles_hbm, prior_hbm, running,
@@ -183,11 +185,11 @@
         return pltpu.VMEM((2 * (-(-levels * count // 16) * 16), width), jnp.float32)
 
     low_a, up_a, lifted = pl.pallas_call(
-        functools.partial(early_kernel, "col", 0, thin, wide, parts),
+        functools.partial(early_kernel, "col", 0, thin, wide, blocks, parts),
         out_shape=[rim(wide), rim(wide), jax.ShapeDtypeStruct(adjoint_in.shape, jnp.bfloat16)],
         in_specs=[SMEM, SMEM, VMEM, VMEM, HBM],
         out_specs=[VMEM, VMEM, VMEM],
-        scratch_shapes=[tile_scratch, rim_running(wide), *lists, pltpu.SemaphoreType.DMA((parts,))],
+        scratch_shapes=[tile_scratch, rim_running(blocks), *lists, pltpu.SemaphoreType.DMA((parts,))],
         compiler_params=params,
         cost_estimate=cost,
         name="early",
@@ -195,7 +197,7 @@
     low_a = shift(low_a, "col", -1)
     up_a = shift(up_a, "col", 1)
     low_b, up_b = pl.pallas_call(
-        functools.partial(late_kernel, "col", wide, 0, thin, parts),
+        functools.partial(late_kernel, "col", wide, 0, thin, thin, parts),
         out_shape=[rim(thin), rim(thin)],
         in_specs=[SMEM, SMEM, VMEM, HBM],
         out_specs=[VMEM, VMEM],

time: 33.6 us -> 32.2 us (0.958); the launches traced: 33.9 us -> 32 us
  Pallas kernels: 16.3 us -> 15 us
  starting transfers between devices: 10.9 us -> 9.99 us
  waiting for transfers between devices: 2.71 us -> 3.08 us
    ppermute x4, starting transfers between devices: 10.9 us -> 9.99 us  [shift(): lax.ppermute(value, axis, [(i, (i + steps) % count) for i in range(count)])]
    pallas_call x2, Pallas kernels: 10.3 us -> 9.4 us  [the longest x1 4.75 us: local(): pl.pallas_call(functools.partial(early_kernel, 'col', 0, thin, wide, bloc...]
    ppermute x4, waiting for transfers between devices: 2.71 us -> 3.08 us  [shift(): lax.ppermute(value, axis, [(i, (i + steps) % count) for i in range(count)])]
    pallas_call x1, Pallas kernels: 5.97 us -> 5.6 us  [local(): pl.pallas_call(functools.partial(middle_kernel, 'col', parts), out_shape=...]
  transfers between devices with their start and end apart: 4 -> 4, of which waited for: 1 -> 1; matrix products, arithmetic and copies ran while one was open for 0% -> 0% of each run, Pallas kernels for 31% -> 32%
where the time goes in v3:
time: 32.2 us; the launch traced here: 32 us
  Pallas kernels  15 us (47%)
  starting transfers between devices  9.99 us (31%)
  waiting for transfers between devices  3.08 us (10%)
  local copies, waits for them, and re-layouts  2.38 us (7%)
  other arithmetic  1.5 us (5%)
    ppermute x4, starting transfers between devices, shift(): lax.ppermute(value, axis, [(i, (i + steps) % count) for i in range(count)])  9.99 us
    pallas_call x1, Pallas kernels, local(): pl.pallas_call(functools.partial(middle_kernel, 'col', parts), out_shape=...  5.6 us
    pallas_call x1, Pallas kernels, local(): pl.pallas_call(functools.partial(early_kernel, 'col', 0, thin, wide, bloc...  4.75 us
    pallas_call x1, Pallas kernels, local(): pl.pallas_call(functools.partial(late_kernel, 'col', wide, 0, thin, thin,...  4.65 us
    ppermute x4, waiting for transfers between devices, shift(): lax.ppermute(value, axis, [(i, (i + steps) % count) for i in range(count)])  3.08 us
    unnamed x10, local copies, waits for them, and re-layouts  2.38 us
    transpose x1, other arithmetic, local(): return total.transpose(1, 0, 2)  1.5 us
  transfers between devices with their start and end apart: 4, of which 1 were waited for; matrix products, arithmetic and copies ran while one was open for 0% of the time, Pallas kernels for 32%

profile of v3, /device:TPU:0, one launch (start us, length us, event | category | flops | bytes accessed | tf_op | source)
XLA Modules:
  0.0 32.0 jit_solution(3634303795924438594)
XLA Ops:
  0.0 0.0 copy-start.3
  0.0 1.4 %copy.7.a = bf16[24,137,128]{2,1,0:T(8,128)(2,1)S(1)} copy(bf16[24,137,128]{2,0,1:T(8,128)(2,1)} %param.6) | data formatting | bytes 1683456 | tf_op args[0]
  1.4 0.3 copy-done.3
  1.7 0.0 copy-start.1
  1.7 0.0 copy-start.2
  1.7 0.3 %copy.8.v = bf16[24,137,137]{2,1,0:T(8,128)(2,1)S(1)} copy(bf16[24,137,137]{2,0,1:T(8,128)(2,1)S(1)} %copy-done.3) | data formatting | bytes 1801824 | tf_op args[1]
  2.1 0.3 %copy-done.1 = s32[24,8]{0,1:T(8,128)S(1)} copy-done((s32[24,8]{0,1:T(8,128)S(1)}, s32[24,8]{0,1:T(8,128)}, u32[]{:S(2)}) %copy-start.1) | copy-done | bytes 792
  2.4 0.0 copy-done.2
  2.4 4.8 %early.1 = (bf16[2192,128]{1,0:T(8,128)(2,1)S(1)}, bf16[2192,128]{1,0:T(8,128)(2,1)S(1)}, bf16[24,137,128]{2,1,0:T(8,128)(2,1)S(1)}) custom-call(s32[8,24]{1,0:T(8,128)S(1)} %bitcast.14, s32[24]{0:T(128)S(1)} %copy-done.2, bf16[24,137,128]{2,1,0:T(8,128)(2,1)S(1)} %copy.7.a, bf16[24,137,137]{2,1,0:T(8,128)(2,1)S(1)} %copy.8.v, bf16[192,128,128]{2,1,0:T(8,128)(2,1)} %bitcast.17), custom_call_target="tpu_custom_call" | custom-call | flops 400000000 | bytes 8000000 | tf_op jit(solution)/shard_map/early/pallas_call | solution.py:187
  7.2 5.5 %collective-permute-start = (bf16[2192,128]{1,0:T(8,128)(2,1)S(1)}, bf16[2192,128]{1,0:T(8,128)(2,1)S(1)}, u32[]{:S(2)}, u32[]{:S(2)}) collective-permute-start(bf16[2192,128]{1,0:T(8,128)(2,1)S(1)} %get-tuple-element.11), channel_id=1, source_target_pairs={{0,15},{1,0},{2,1},{3,2},{4,3},{5,4},{6,5},{7,6},{8,7},{9,8},{10,9... | collective-permute-start | bytes 1683464 | tf_op jit(solution)/shard_map/ppermute | solution.py:164
  12.6 0.0 collective-permute-start.3
  12.7 0.0 copy-start
  12.7 4.6 %late.1 = (bf16[1096,128]{1,0:T(8,128)(2,1)S(1)}, bf16[1096,128]{1,0:T(8,128)(2,1)S(1)}) custom-call(s32[8,24]{1,0:T(8,128)S(1)} %bitcast.15, s32[24]{0:T(128)S(1)} %copy-done.2, bf16[24,137,128]{2,1,0:T(8,128)(2,1)S(1)} %get-tuple-element.10.lifted, bf16[192,128,128]{2,1,0:T(8,128)(2,1)} %bitcast.18), custom_call_target="tpu_custom_call" | custom-call | flops 400000000 | bytes 8000000 | tf_op jit(solution)/shard_map/late/pallas_call | solution.py:199
  17.3 4.5 %collective-permute-start.1 = (bf16[1096,128]{1,0:T(8,128)(2,1)S(1)}, bf16[1096,128]{1,0:T(8,128)(2,1)S(1)}, u32[]{:S(2)}, u32[]{:S(2)}) collective-permute-start(bf16[1096,128]{1,0:T(8,128)(2,1)S(1)} %get-tuple-element.12), channel_id=1, source_target_pairs={{0,15},{1,0},{2,1},{3,2},{4,3},{5,4},{6,5},{7,6},{8,7},{9,8},{10,9... | collective-permute-start | bytes 841736 | tf_op jit(solution)/shard_map/ppermute | solution.py:164
  21.8 0.0 collective-permute-start.2
  21.8 0.0 copy-done
  21.8 5.6 %middle.1 = f32[3288,128]{1,0:T(8,128)S(1)} custom-call(s32[8,24]{1,0:T(8,128)S(1)} %bitcast.16, s32[24]{0:T(128)S(1)} %copy-done.2, bf16[24,137,128]{2,1,0:T(8,128)(2,1)S(1)} %get-tuple-element.10.lifted, bf16[192,128,128]{2,1,0:T(8,128)(2,1)} %bitcast.19, f32[3288,128]{1,0:T(8,128)S(1)} %bitcast.13), custom_call_target="tpu_custom_call" | custom-call | flops 400000000 | bytes 8000000 | tf_op jit(solution)/shard_map/middle/pallas_call | solution.py:211
  27.4 0.0 collective-permute-done.1
  27.4 3.1 %collective-permute-done.2 = bf16[1096,128]{1,0:T(8,128)(2,1)S(1)} collective-permute-done((bf16[1096,128]{1,0:T(8,128)(2,1)S(1)}, bf16[1096,128]{1,0:T(8,128)(2,1)S(1)}, u32[]{:S(2)}, u32[]{:S(2)}) %collective-permute-start.2) | collective-permute-done | bytes 280608 | tf_op jit(solution)/shard_map/ppermute | solution.py:164
  30.5 0.0 collective-permute-done
  30.5 0.0 collective-permute-done.3
  30.5 1.5 %add_bitcast_fusion = f32[24,137,128]{2,0,1:T(8,128)} fusion(f32[137,24,128]{2,1,0:T(8,128)S(1)} %bitcast.12, bf16[137,8,128]{2,1,0:T(8,128)(2,1)S(1)} %bitcast.22, bf16[137,16,128]{2,1,0:T(8,128)(2,1)S(1)} %bitcast.20, bf16[137,16,128]{2,1,0:T(8,128)(2,1)S(1)} %bitcast.21, bf16[137,8,128]{2,1,0:T(8,128)(2,1)S(1)} %bitcast.23), kind=kLoop, calls=%fused_computation | loop fusion | flops 4208640 | bytes 5050368 | tf_op jit(solution)/shard_map/transpose | solution.py:227
Async XLA Ops:
  0.0 1.7 %copy-start.3 = (bf16[24,137,137]{2,0,1:T(8,128)(2,1)S(1)}, bf16[24,137,137]{2,0,1:T(8,128)(2,1)}, u32[]{:S(2)}) copy-start(bf16[24,137,137]{2,0,1:T(8,128)(2,1)} %param.7) | copy-start | bytes 2702740
  1.7 0.7 %copy-start.1 = (s32[24,8]{0,1:T(8,128)S(1)}, s32[24,8]{0,1:T(8,128)}, u32[]{:S(2)}) copy-start(s32[24,8]{0,1:T(8,128)} %param.9) | copy-start | bytes 2308
  1.7 0.7 %copy-start.2 = (s32[24]{0:T(128)S(1)}, s32[24]{0:T(128)}, u32[]{:S(2)}) copy-start(s32[24]{0:T(128)} %len_ref.5) | copy-start | bytes 292
  7.2 23.3 %collective-permute-start = (bf16[2192,128]{1,0:T(8,128)(2,1)S(1)}, bf16[2192,128]{1,0:T(8,128)(2,1)S(1)}, u32[]{:S(2)}, u32[]{:S(2)}) collective-permute-start(bf16[2192,128]{1,0:T(8,128)(2,1)S(1)} %get-tuple-element.11), channel_id=1, source_target_pairs={{0,15},{1,0},{2,1},{3,2},{4,3},{5,4},{6,5},{7,6},{8,7},{9,8},{10,9... | collective-permute-start | bytes 1683464 | tf_op jit(solution)/shard_map/ppermute | solution.py:164
  12.6 17.8 %collective-permute-start.3 = (bf16[2192,128]{1,0:T(8,128)(2,1)S(1)}, bf16[2192,128]{1,0:T(8,128)(2,1)S(1)}, u32[]{:S(2)}, u32[]{:S(2)}) collective-permute-start(bf16[2192,128]{1,0:T(8,128)(2,1)S(1)} %get-tuple-element.14), channel_id=1, source_target_pairs={{0,1},{1,2},{2,3},{3,4},{4,5},{5,6},{6,7},{7,8},{8,9},{9,10},{10,1... | collective-permute-start | bytes 1683464 | tf_op jit(solution)/shard_map/ppermute | solution.py:164
  12.7 9.1 %copy-start = (f32[24,137,128]{2,0,1:T(8,128)S(1)}, f32[24,137,128]{2,0,1:T(8,128)}, u32[]{:S(2)}) copy-start(f32[24,137,128]{2,0,1:T(8,128)} %param.11) | copy-start | bytes 5050372
  17.3 10.1 %collective-permute-start.1 = (bf16[1096,128]{1,0:T(8,128)(2,1)S(1)}, bf16[1096,128]{1,0:T(8,128)(2,1)S(1)}, u32[]{:S(2)}, u32[]{:S(2)}) collective-permute-start(bf16[1096,128]{1,0:T(8,128)(2,1)S(1)} %get-tuple-element.12), channel_id=1, source_target_pairs={{0,15},{1,0},{2,1},{3,2},{4,3},{5,4},{6,5},{7,6},{8,7},{9,8},{10,9... | collective-permute-start | bytes 841736 | tf_op jit(solution)/shard_map/ppermute | solution.py:164
  21.8 8.7 %collective-permute-start.2 = (bf16[1096,128]{1,0:T(8,128)(2,1)S(1)}, bf16[1096,128]{1,0:T(8,128)(2,1)S(1)}, u32[]{:S(2)}, u32[]{:S(2)}) collective-permute-start(bf16[1096,128]{1,0:T(8,128)(2,1)S(1)} %get-tuple-element.13), channel_id=1, source_target_pairs={{0,1},{1,2},{2,3},{3,4},{4,5},{5,6},{6,7},{7,8},{8,9},{9,10},{10,1... | collective-permute-start | bytes 841736 | tf_op jit(solution)/shard_map/ppermute | solution.py:164

commit v4 on v3

--- a/solution.py
+++ b/solution.py
@@ -8,7 +8,7 @@
 from jax.sharding import PartitionSpec as P
 
 GROUP = 8
-UNROLL = 4
+UNROLL = 8
 FIRST = 16
 VMEM_BYTES = 48 << 20
 

time: 32.2 us -> 32.3 us (level)
  starting transfers between devices: 9.99 us -> 10.4 us
    ppermute x4, starting transfers between devices: 9.99 us -> 10.4 us  [shift(): lax.ppermute(value, axis, [(i, (i + steps) % count) for i in range(count)])]
where the time goes in v4:
time: 32.3 us
  Pallas kernels  14.9 us (46%)
  starting transfers between devices  10.4 us (32%)
  waiting for transfers between devices  3.1 us (10%)
  local copies, waits for them, and re-layouts  2.38 us (7%)
  other arithmetic  1.5 us (5%)
    ppermute x4, starting transfers between devices, shift(): lax.ppermute(value, axis, [(i, (i + steps) % count) for i in range(count)])  10.4 us
    pallas_call x1, Pallas kernels, local(): pl.pallas_call(functools.partial(middle_kernel, 'col', parts), out_shape=...  5.59 us
    pallas_call x1, Pallas kernels, local(): pl.pallas_call(functools.partial(early_kernel, 'col', 0, thin, wide, bloc...  4.7 us
    pallas_call x1, Pallas kernels, local(): pl.pallas_call(functools.partial(late_kernel, 'col', wide, 0, thin, thin,...  4.65 us
    ppermute x4, waiting for transfers between devices, shift(): lax.ppermute(value, axis, [(i, (i + steps) % count) for i in range(count)])  3.1 us
    unnamed x10, local copies, waits for them, and re-layouts  2.38 us
    transpose x1, other arithmetic, local(): return total.transpose(1, 0, 2)  1.5 us
  transfers between devices with their start and end apart: 4, of which 1 were waited for; matrix products, arithmetic and copies ran while one was open for 0% of the time, Pallas kernels for 32%

profile of v4, /device:TPU:0, one launch (start us, length us, event | category | flops | bytes accessed | tf_op | source)
XLA Modules:
  0.0 32.3 jit_solution(1331786333303462407)
XLA Ops:
  0.0 0.0 copy-start.3
  0.0 1.4 %copy.7.a = bf16[24,137,128]{2,1,0:T(8,128)(2,1)S(1)} copy(bf16[24,137,128]{2,0,1:T(8,128)(2,1)} %param.6) | data formatting | bytes 1683456 | tf_op args[0]
  1.4 0.3 copy-done.3
  1.7 0.0 copy-start.1
  1.7 0.0 copy-start.2
  1.7 0.3 %copy.8.v = bf16[24,137,137]{2,1,0:T(8,128)(2,1)S(1)} copy(bf16[24,137,137]{2,0,1:T(8,128)(2,1)S(1)} %copy-done.3) | data formatting | bytes 1801824 | tf_op args[1]
  2.1 0.3 %copy-done.1 = s32[24,8]{0,1:T(8,128)S(1)} copy-done((s32[24,8]{0,1:T(8,128)S(1)}, s32[24,8]{0,1:T(8,128)}, u32[]{:S(2)}) %copy-start.1) | copy-done | bytes 792
  2.4 0.0 copy-done.2
  2.4 4.7 %early.1 = (bf16[2192,128]{1,0:T(8,128)(2,1)S(1)}, bf16[2192,128]{1,0:T(8,128)(2,1)S(1)}, bf16[24,137,128]{2,1,0:T(8,128)(2,1)S(1)}) custom-call(s32[8,24]{1,0:T(8,128)S(1)} %bitcast.14, s32[24]{0:T(128)S(1)} %copy-done.2, bf16[24,137,128]{2,1,0:T(8,128)(2,1)S(1)} %copy.7.a, bf16[24,137,137]{2,1,0:T(8,128)(2,1)S(1)} %copy.8.v, bf16[192,128,128]{2,1,0:T(8,128)(2,1)} %bitcast.17), custom_call_target="tpu_custom_call" | custom-call | flops 400000000 | bytes 8000000 | tf_op jit(solution)/shard_map/early/pallas_call | solution.py:187
  7.1 5.5 %collective-permute-start = (bf16[2192,128]{1,0:T(8,128)(2,1)S(1)}, bf16[2192,128]{1,0:T(8,128)(2,1)S(1)}, u32[]{:S(2)}, u32[]{:S(2)}) collective-permute-start(bf16[2192,128]{1,0:T(8,128)(2,1)S(1)} %get-tuple-element.11), channel_id=1, source_target_pairs={{0,15},{1,0},{2,1},{3,2},{4,3},{5,4},{6,5},{7,6},{8,7},{9,8},{10,9... | collective-permute-start | bytes 1683464 | tf_op jit(solution)/shard_map/ppermute | solution.py:164
  12.6 0.0 collective-permute-start.3
  12.6 0.0 copy-start
  12.6 4.6 %late.1 = (bf16[1096,128]{1,0:T(8,128)(2,1)S(1)}, bf16[1096,128]{1,0:T(8,128)(2,1)S(1)}) custom-call(s32[8,24]{1,0:T(8,128)S(1)} %bitcast.15, s32[24]{0:T(128)S(1)} %copy-done.2, bf16[24,137,128]{2,1,0:T(8,128)(2,1)S(1)} %get-tuple-element.10.lifted, bf16[192,128,128]{2,1,0:T(8,128)(2,1)} %bitcast.18), custom_call_target="tpu_custom_call" | custom-call | flops 400000000 | bytes 8000000 | tf_op jit(solution)/shard_map/late/pallas_call | solution.py:199
  17.3 4.9 %collective-permute-start.1 = (bf16[1096,128]{1,0:T(8,128)(2,1)S(1)}, bf16[1096,128]{1,0:T(8,128)(2,1)S(1)}, u32[]{:S(2)}, u32[]{:S(2)}) collective-permute-start(bf16[1096,128]{1,0:T(8,128)(2,1)S(1)} %get-tuple-element.12), channel_id=1, source_target_pairs={{0,15},{1,0},{2,1},{3,2},{4,3},{5,4},{6,5},{7,6},{8,7},{9,8},{10,9... | collective-permute-start | bytes 841736 | tf_op jit(solution)/shard_map/ppermute | solution.py:164
  22.1 0.0 collective-permute-start.2
  22.1 0.0 copy-done
  22.1 5.6 %middle.1 = f32[3288,128]{1,0:T(8,128)S(1)} custom-call(s32[8,24]{1,0:T(8,128)S(1)} %bitcast.16, s32[24]{0:T(128)S(1)} %copy-done.2, bf16[24,137,128]{2,1,0:T(8,128)(2,1)S(1)} %get-tuple-element.10.lifted, bf16[192,128,128]{2,1,0:T(8,128)(2,1)} %bitcast.19, f32[3288,128]{1,0:T(8,128)S(1)} %bitcast.13), custom_call_target="tpu_custom_call" | custom-call | flops 400000000 | bytes 8000000 | tf_op jit(solution)/shard_map/middle/pallas_call | solution.py:211
  27.7 0.0 collective-permute-done.1
  27.7 3.1 %collective-permute-done.2 = bf16[1096,128]{1,0:T(8,128)(2,1)S(1)} collective-permute-done((bf16[1096,128]{1,0:T(8,128)(2,1)S(1)}, bf16[1096,128]{1,0:T(8,128)(2,1)S(1)}, u32[]{:S(2)}, u32[]{:S(2)}) %collective-permute-start.2) | collective-permute-done | bytes 280608 | tf_op jit(solution)/shard_map/ppermute | solution.py:164
  30.8 0.0 collective-permute-done
  30.8 0.0 collective-permute-done.3
  30.8 1.5 %add_bitcast_fusion = f32[24,137,128]{2,0,1:T(8,128)} fusion(f32[137,24,128]{2,1,0:T(8,128)S(1)} %bitcast.12, bf16[137,8,128]{2,1,0:T(8,128)(2,1)S(1)} %bitcast.22, bf16[137,16,128]{2,1,0:T(8,128)(2,1)S(1)} %bitcast.20, bf16[137,16,128]{2,1,0:T(8,128)(2,1)S(1)} %bitcast.21, bf16[137,8,128]{2,1,0:T(8,128)(2,1)S(1)} %bitcast.23), kind=kLoop, calls=%fused_computation | loop fusion | flops 4208640 | bytes 5050368 | tf_op jit(solution)/shard_map/transpose | solution.py:227
Async XLA Ops:
  0.0 1.7 %copy-start.3 = (bf16[24,137,137]{2,0,1:T(8,128)(2,1)S(1)}, bf16[24,137,137]{2,0,1:T(8,128)(2,1)}, u32[]{:S(2)}) copy-start(bf16[24,137,137]{2,0,1:T(8,128)(2,1)} %param.7) | copy-start | bytes 2702740
  1.7 0.7 %copy-start.1 = (s32[24,8]{0,1:T(8,128)S(1)}, s32[24,8]{0,1:T(8,128)}, u32[]{:S(2)}) copy-start(s32[24,8]{0,1:T(8,128)} %param.9) | copy-start | bytes 2308
  1.7 0.7 %copy-start.2 = (s32[24]{0:T(128)S(1)}, s32[24]{0:T(128)}, u32[]{:S(2)}) copy-start(s32[24]{0:T(128)} %len_ref.5) | copy-start | bytes 292
  7.1 23.7 %collective-permute-start = (bf16[2192,128]{1,0:T(8,128)(2,1)S(1)}, bf16[2192,128]{1,0:T(8,128)(2,1)S(1)}, u32[]{:S(2)}, u32[]{:S(2)}) collective-permute-start(bf16[2192,128]{1,0:T(8,128)(2,1)S(1)} %get-tuple-element.11), channel_id=1, source_target_pairs={{0,15},{1,0},{2,1},{3,2},{4,3},{5,4},{6,5},{7,6},{8,7},{9,8},{10,9... | collective-permute-start | bytes 1683464 | tf_op jit(solution)/shard_map/ppermute | solution.py:164
  12.6 18.2 %collective-permute-start.3 = (bf16[2192,128]{1,0:T(8,128)(2,1)S(1)}, bf16[2192,128]{1,0:T(8,128)(2,1)S(1)}, u32[]{:S(2)}, u32[]{:S(2)}) collective-permute-start(bf16[2192,128]{1,0:T(8,128)(2,1)S(1)} %get-tuple-element.14), channel_id=1, source_target_pairs={{0,1},{1,2},{2,3},{3,4},{4,5},{5,6},{6,7},{7,8},{8,9},{9,10},{10,1... | collective-permute-start | bytes 1683464 | tf_op jit(solution)/shard_map/ppermute | solution.py:164
  12.6 9.5 %copy-start = (f32[24,137,128]{2,0,1:T(8,128)S(1)}, f32[24,137,128]{2,0,1:T(8,128)}, u32[]{:S(2)}) copy-start(f32[24,137,128]{2,0,1:T(8,128)} %param.11) | copy-start | bytes 5050372
  17.3 10.5 %collective-permute-start.1 = (bf16[1096,128]{1,0:T(8,128)(2,1)S(1)}, bf16[1096,128]{1,0:T(8,128)(2,1)S(1)}, u32[]{:S(2)}, u32[]{:S(2)}) collective-permute-start(bf16[1096,128]{1,0:T(8,128)(2,1)S(1)} %get-tuple-element.12), channel_id=1, source_target_pairs={{0,15},{1,0},{2,1},{3,2},{4,3},{5,4},{6,5},{7,6},{8,7},{9,8},{10,9... | collective-permute-start | bytes 841736 | tf_op jit(solution)/shard_map/ppermute | solution.py:164
  22.1 8.7 %collective-permute-start.2 = (bf16[1096,128]{1,0:T(8,128)(2,1)S(1)}, bf16[1096,128]{1,0:T(8,128)(2,1)S(1)}, u32[]{:S(2)}, u32[]{:S(2)}) collective-permute-start(bf16[1096,128]{1,0:T(8,128)(2,1)S(1)} %get-tuple-element.13), channel_id=1, source_target_pairs={{0,1},{1,2},{2,3},{3,4},{4,5},{5,6},{6,7},{7,8},{8,9},{9,10},{10,1... | collective-permute-start | bytes 841736 | tf_op jit(solution)/shard_map/ppermute | solution.py:164
